TPU v7x, 32 devices: a whole 2x2x4 slice. The times are simulated.
32 devices in a mesh: gx: 4 (over z), gy: 8 (over y, x, core).
Axes of the slice: x: 2, y: 2, z: 4, core: 2. Of those that a mesh axis runs over, the one named last changes fastest.
Arguments:
- pixel_adjoint: float32 [4, 32, 4096], P(None, None, ('gx', 'gy')), may hold values from -6 to 6
- pixel_owner: int32 [4, 4096, 1], P(None, ('gx', 'gy')), may hold values from 0 to 31; in each aligned block of 128 rows (0 to 127, 128 to 255, ..., all dimensions but the last counted through in order) at most 8 rows name the same one
- pixel_column: int32 [4, 4096], P(None, ('gx', 'gy')), may hold values from 0 to 1023
- pixel_level: int32 [4, 4096], P(None, ('gx', 'gy')), may hold values from 0 to 24
- wind_x: float32 [4, 32, 1024], P(None, 'gx', 'gy'), may hold values from -0.45 to 0.45
- wind_y: float32 [4, 32, 1024], P(None, 'gx', 'gy'), may hold values from -0.45 to 0.45
- diffusivity: float32 [39, 32, 1024], P(None, 'gx', 'gy'), may hold values from 0.1 to 10
- prior_emission: float32 [2, 32, 1024], P(None, 'gx', 'gy'), may hold values from 0.01 to 0.1
- region_map: int32 [32, 1024], P('gx', 'gy'), may hold values from 0 to 255, as said below
Outputs:
- adjoint_out: float32 [2, 40, 32, 1024], P(None, None, 'gx', 'gy')
- emission_gradient: float32 [2, 256], P(None, ('gx', 'gy'))
Inputs may be any that keep to these rules, and one draw needn't show every extreme that they name: `pixel_owner`: within the 128 entries of one device in one step no owner is named more than 8 times, a bound that some block reaches. `region_map`: constant on aligned blocks of 2 rows by 4 columns; every region covers exactly 16 such blocks.
All inputs are finite; a program needn't handle non-finite values.
Results may differ from a plain program's by a relative error of at most 0.00014.
Values sent between devices are 32-bit elements; how exact they have to be, the bound alone decides.
A program may use at most 64 MiB of HBM per device.

v0:
```python
import functools

import jax
import jax.numpy as jnp
from jax import lax
from jax.experimental import pallas as pl
from jax.experimental.pallas import tpu as pltpu
from jax.sharding import PartitionSpec as P

REG_DEV = 8
MESH = pl.DeviceIdType.MESH
F32 = jnp.float32
BF16 = jnp.bfloat16


def halves(value):
    high = value.astype(BF16)
    low = (value - high.astype(F32)).astype(BF16)
    return high, low


def dot_nt(a, b):
    return lax.dot_general(a, b, (((1,), (1,)), ((), ())), preferred_element_type=F32)


def kernel(
    dims,
    adj_ref,
    owner_ref,
    column_ref,
    level_ref,
    wx_ref,
    wy_ref,
    diff_ref,
    prior_ref,
    region_ref,
    state,
    grad_ref,
    table,
    send,
    recv,
    inv_ref,
    coup_ref,
    ratio_ref,
    forcing,
    forced,
    moved,
    row_out,
    row_in,
    col_out,
    col_in,
    surf,
    gsend,
    grecv,
    pix_send,
    pix_recv,
    halo_send,
    halo_recv,
    g_send,
    g_recv,
):
    nx, ny, species, levels, akl, steps, rows, cols, pixels, slots = dims
    n = nx * ny
    planes = species * levels
    gx, gy = lax.axis_index("gx"), lax.axis_index("gy")
    me = gx * ny + gy

    def partner(i):
        other = lax.rem(me + i, n)
        return other, (lax.div(other, ny), lax.rem(other, ny))

    row_in[...] = jnp.zeros(row_in.shape, F32)
    col_in[...] = jnp.zeros(col_in.shape, F32)
    barrier = pltpu.get_barrier_semaphore()

    def greet(i, carry):
        other, place = partner(i)
        pl.semaphore_signal(barrier, inc=1, device_id=place, device_id_type=MESH)
        return carry

    lax.fori_loop(1, n, greet, 0)

    def pack(k):
        table[...] = jnp.zeros((128, pixels), F32)
        for s in range(species):
            table[s * levels : s * levels + akl, :] = adj_ref[k, s * akl : (s + 1) * akl, :]
        table[planes : planes + 1, :] = column_ref[k : k + 1, :].astype(F32)
        table[planes + 1 : planes + 2, :] = level_ref[k : k + 1, :].astype(F32)
        owner = owner_ref[k : k + 1, :].astype(F32)
        along = jnp.broadcast_to(owner, (pixels, pixels))
        down = along.T
        first = lax.broadcasted_iota(jnp.int32, (pixels, pixels), 0)
        second = lax.broadcasted_iota(jnp.int32, (pixels, pixels), 1)
        earlier = jnp.where((along == down) & (first < second), 1.0, 0.0)
        slot = jnp.sum(earlier, axis=0, keepdims=True)
        position = (owner * slots + slot).astype(jnp.int32)
        place = lax.broadcasted_iota(jnp.int32, (n * slots, pixels), 0)
        hits = jnp.where(place == position, 1.0, 0.0).astype(BF16)
        high, low = halves(table[...])
        send[k] = dot_nt(hits, high) + dot_nt(hits, low)

    def pixel_copy(k, i):
        other, place = partner(i)
        return pltpu.make_async_remote_copy(
            src_ref=send.at[k, pl.ds(pl.multiple_of(other * slots, slots), slots)],
            dst_ref=recv.at[k, pl.ds(pl.multiple_of(me * slots, slots), slots)],
            send_sem=pix_send.at[k],
            recv_sem=pix_recv.at[k],
            device_id=place,
            device_id_type=MESH,
        )

    def pixel_all(k):
        _, place = partner(1)
        part = pl.ds(0, (n - 1) * slots)
        return pltpu.make_async_remote_copy(
            src_ref=send.at[k, part],
            dst_ref=recv.at[k, part],
            send_sem=pix_send.at[k],
            recv_sem=pix_recv.at[k],
            device_id=place,
            device_id_type=MESH,
        )

    def send_pixels(k):
        def go(i, carry):
            pixel_copy(k, i).start()
            return carry

        lax.fori_loop(1, n, go, 0)
        mine = pl.ds(pl.multiple_of(me * slots, slots), slots)
        recv[k, mine, :] = send[k, mine, :]

    pack(steps - 1)
    pl.semaphore_wait(barrier, n - 1)
    send_pixels(steps - 1)
    for k in reversed(range(steps - 1)):
        pack(k)
        send_pixels(k)

    ratio = jnp.zeros((rows, cols), F32)
    for level in range(levels):
        below = diff_ref[level - 1] if level else jnp.zeros((rows, cols), F32)
        above = diff_ref[level] if level < levels - 1 else jnp.zeros((rows, cols), F32)
        inverse = 1.0 / (1.0 + below + above + below * ratio)
        ratio = -above * inverse
        here = slice(level * rows, (level + 1) * rows)
        inv_ref[here, :] = inverse
        coup_ref[here, :] = below * inverse
        ratio_ref[here, :] = ratio
    surf[...] = jnp.zeros(surf.shape, F32)
    state[...] = jnp.zeros(state.shape, F32)

    lane = lax.broadcasted_iota(jnp.int32, (rows, cols), 1)
    sub = lax.broadcasted_iota(jnp.int32, (rows, cols), 0)

    def spread(k):
        pixel_all(k).wait_recv()
        total = [None] * rows
        chunk = min(256, n * slots)
        for first in range(0, n * slots, chunk):
            got = recv[k, first : first + chunk, :]
            spot = lax.broadcasted_iota(jnp.int32, got.shape, 1)
            column = jnp.broadcast_to(got[:, planes : planes + 1], got.shape).astype(jnp.int32)
            level = jnp.broadcast_to(got[:, planes + 1 : planes + 2], got.shape).astype(jnp.int32)
            profile = jnp.where(spot < planes, got, 0.0)
            bit = 1
            while bit <= levels - akl:
                profile = jnp.where((level & bit) != 0, pltpu.roll(profile, bit, 1), profile)
                bit *= 2
            high, low = halves(profile.T[:planes])
            both = jnp.concatenate([high, low], axis=0)
            for x in range(0, rows, 2):
                hits = jnp.concatenate(
                    [
                        jnp.where(column == spot + (x + d) * cols, 1.0, 0.0).astype(BF16)
                        for d in range(2)
                    ],
                    axis=1,
                )
                out = jnp.dot(both, hits, preferred_element_type=F32)
                out = out[:planes] + out[planes:]
                for d in range(2):
                    piece = out[:, d * cols : (d + 1) * cols]
                    total[x + d] = piece if total[x + d] is None else total[x + d] + piece
        for x in range(rows):
            forcing[pl.ds(x, planes, stride=rows), :] = total[x]

    has = (gx < nx - 1, gx > 0, gy < ny - 1, gy > 0)
    comes = (gx > 0, gx < nx - 1, gy > 0, gy < ny - 1)
    goes = (
        (jnp.minimum(gx + 1, nx - 1), gy),
        (jnp.maximum(gx - 1, 0), gy),
        (gx, jnp.minimum(gy + 1, ny - 1)),
        (gx, jnp.maximum(gy - 1, 0)),
    )

    def halo(k, side):
        source, target = (row_out, row_in) if side < 2 else (col_out, col_in)
        return pltpu.make_async_remote_copy(
            src_ref=source.at[k, side % 2],
            dst_ref=target.at[k, side % 2],
            send_sem=halo_send.at[k, side],
            recv_sem=halo_recv.at[k, side],
            device_id=goes[side],
            device_id_type=MESH,
        )

    spread(steps - 1)

    def step(turn, carry):
        k = steps - 1 - turn
        wx, wy = wx_ref[k], wy_ref[k]
        ahead_x, back_x = jnp.maximum(-wx, 0.0), jnp.maximum(wx, 0.0)
        ahead_y, back_y = jnp.maximum(-wy, 0.0), jnp.maximum(wy, 0.0)
        forced[...] = state[...] + forcing[...]
        row_out[k, 0] = forced[pl.ds(rows - 1, planes, stride=rows), :] * ahead_x[rows - 1 : rows]
        row_out[k, 1] = forced[pl.ds(0, planes, stride=rows), :] * back_x[0:1]
        for side in (0, 1):
            pl.when(has[side])(lambda side=side: halo(k, side).start())
        up = jnp.zeros((rows, cols), F32)
        down = jnp.zeros((rows, cols), F32)
        for j in range(planes):
            cell = forced[j * rows : (j + 1) * rows, :]
            up = jnp.where(lane == j, pltpu.roll(ahead_y * cell, (j + 1) % cols, 1), up)
            down = jnp.where(lane == j, pltpu.roll(back_y * cell, j, 1) if j else back_y * cell, down)
        col_out[k, 0] = up
        col_out[k, 1] = down
        for side in (2, 3):
            pl.when(has[side])(lambda side=side: halo(k, side).start())
        remain = 1.0 - (ahead_x + back_x + ahead_y + back_y)
        ahead_x_in = jnp.where(sub > 0, pltpu.roll(ahead_x, 1, 0), 0.0)
        back_x_in = jnp.where(sub < rows - 1, pltpu.roll(back_x, rows - 1, 0), 0.0)
        ahead_y_in = jnp.where(lane > 0, pltpu.roll(ahead_y, 1, 1), 0.0)
        back_y_in = jnp.where(lane < cols - 1, pltpu.roll(back_y, cols - 1, 1), 0.0)
        for j in range(planes):
            cell = forced[j * rows : (j + 1) * rows, :]
            moved[j * rows : (j + 1) * rows, :] = (
                cell * remain
                + ahead_x_in * pltpu.roll(cell, 1, 0)
                + back_x_in * pltpu.roll(cell, rows - 1, 0)
                + ahead_y_in * pltpu.roll(cell, 1, 1)
                + back_y_in * pltpu.roll(cell, cols - 1, 1)
            )

        @pl.when(k > 0)
        def _():
            spread(jnp.maximum(k - 1, 0))

        for side in range(4):
            pl.when(comes[side])(lambda side=side: halo(k, side).wait_recv())
        moved[pl.ds(0, planes, stride=rows), :] += row_in[k, 0]
        moved[pl.ds(rows - 1, planes, stride=rows), :] += row_in[k, 1]
        up = col_in[k, 0]
        down = col_in[k, 1]
        for s in range(species):
            value = jnp.zeros((rows, cols), F32)
            for level in range(levels):
                j = s * levels + level
                here = slice(j * rows, (j + 1) * rows)
                flat = slice(level * rows, (level + 1) * rows)
                edge = jnp.where(lane == 0, pltpu.roll(up, (cols - j) % cols, 1) if j else up, 0.0)
                edge = jnp.where(lane == cols - 1, pltpu.roll(down, cols - 1 - j, 1), edge)
                value = (moved[here, :] + edge) * inv_ref[flat, :] + coup_ref[flat, :] * value
                moved[here, :] = value
            value = jnp.zeros((rows, cols), F32)
            for level in reversed(range(levels)):
                j = s * levels + level
                here = slice(j * rows, (j + 1) * rows)
                flat = slice(level * rows, (level + 1) * rows)
                value = moved[here, :] - ratio_ref[flat, :] * value
                state[here, :] = value
            surf[s] += prior_ref[s] * value
        return carry

    lax.fori_loop(0, steps, step, 0)

    region = region_ref[...]
    hits, parts = [], []
    sums = [surf[s] + pltpu.roll(surf[s], rows - 1, 0) for s in range(species)]
    for x in range(0, rows, 2):
        reg = region[x : x + 1]
        owner = lax.broadcasted_iota(jnp.int32, (n, cols), 0)
        hits.append(jnp.where(owner == lax.shift_right_logical(reg, 3), 1.0, 0.0).astype(BF16))
        place = lax.broadcasted_iota(jnp.int32, (REG_DEV, cols), 0)
        same = place == (reg & (REG_DEV - 1))
        blocks = [jnp.where(same, sums[s][x : x + 1], 0.0) for s in range(species)]
        blocks.append(jnp.zeros((128 - species * REG_DEV, cols), F32))
        parts.append(jnp.concatenate(blocks, axis=0))
    hits = jnp.concatenate(hits, axis=1)
    high, low = halves(jnp.concatenate(parts, axis=1))
    gsend[...] = (dot_nt(hits, high) + dot_nt(hits, low)).reshape(n, 1, 128)

    def grad_copy(i):
        other, place = partner(i)
        return pltpu.make_async_remote_copy(
            src_ref=gsend.at[other],
            dst_ref=grecv.at[me],
            send_sem=g_send,
            recv_sem=g_recv,
            device_id=place,
            device_id_type=MESH,
        )

    def go(i, carry):
        grad_copy(i).start()
        return carry

    lax.fori_loop(1, n, go, 0)
    grecv[me] = gsend[me]
    for k in range(steps):
        pixel_all(k).wait_send()
        for side in range(4):
            pl.when(has[side])(lambda side=side, k=k: halo(k, side).wait_send())
    _, place = partner(1)
    everything = pltpu.make_async_remote_copy(
        src_ref=gsend.at[pl.ds(0, n - 1)],
        dst_ref=grecv.at[pl.ds(0, n - 1)],
        send_sem=g_send,
        recv_sem=g_recv,
        device_id=place,
        device_id_type=MESH,
    )
    everything.wait_send()
    everything.wait_recv()
    total = jnp.sum(grecv[...], axis=0)
    for s in range(species):
        grad_ref[s : s + 1, :] = total[:, s * REG_DEV : (s + 1) * REG_DEV]


def local(nx, ny, *args):
    adj, owner, column, level, wx, wy, diff, prior, region = args
    steps, rows, cols = wx.shape
    levels, species = diff.shape[0] + 1, prior.shape[0]
    pixels, akl = adj.shape[2], adj.shape[1] // species
    n = nx * ny
    slots = -(-(2 * pixels // n) // 8) * 8
    planes = species * levels
    dims = (nx, ny, species, levels, akl, steps, rows, cols, pixels, slots)
    vmem = pl.BlockSpec(memory_space=pltpu.VMEM)
    tile = (planes * rows, cols)
    state, grad = pl.pallas_call(
        functools.partial(kernel, dims),
        out_shape=(
            jax.ShapeDtypeStruct(tile, F32),
            jax.ShapeDtypeStruct((species, REG_DEV), F32),
        ),
        in_specs=[vmem] * 9,
        out_specs=(vmem, vmem),
        scratch_shapes=[
            pltpu.VMEM((128, pixels), F32),
            pltpu.VMEM((steps, n * slots, 128), F32),
            pltpu.VMEM((steps, n * slots, 128), F32),
            pltpu.VMEM((levels * rows, cols), F32),
            pltpu.VMEM((levels * rows, cols), F32),
            pltpu.VMEM((levels * rows, cols), F32),
            pltpu.VMEM(tile, F32),
            pltpu.VMEM(tile, F32),
            pltpu.VMEM(tile, F32),
            pltpu.VMEM((steps, 2, planes, cols), F32),
            pltpu.VMEM((steps, 2, planes, cols), F32),
            pltpu.VMEM((steps, 2, rows, cols), F32),
            pltpu.VMEM((steps, 2, rows, cols), F32),
            pltpu.VMEM((species, rows, cols), F32),
            pltpu.VMEM((n, 1, 128), F32),
            pltpu.VMEM((n, 1, 128), F32),
            pltpu.SemaphoreType.DMA((steps,)),
            pltpu.SemaphoreType.DMA((steps,)),
            pltpu.SemaphoreType.DMA((steps, 4)),
            pltpu.SemaphoreType.DMA((steps, 4)),
            pltpu.SemaphoreType.DMA,
            pltpu.SemaphoreType.DMA,
        ],
        compiler_params=pltpu.CompilerParams(
            collective_id=0, has_side_effects=True, vmem_limit_bytes=40 * 1024 * 1024
        ),
    )(adj, owner.reshape(steps, pixels), column, level, wx, wy, diff, prior, region)
    return state.reshape(species, levels, rows, cols), grad


def solution(mesh):
    in_specs = (
        P(None, None, ("gx", "gy")),
        P(None, ("gx", "gy"), None),
        P(None, ("gx", "gy")),
        P(None, ("gx", "gy")),
        P(None, "gx", "gy"),
        P(None, "gx", "gy"),
        P(None, "gx", "gy"),
        P(None, "gx", "gy"),
        P("gx", "gy"),
    )
    out_specs = (P(None, None, "gx", "gy"), P(None, ("gx", "gy")))
    body = functools.partial(local, mesh.shape["gx"], mesh.shape["gy"])
    return jax.shard_map(body, mesh=mesh, in_specs=in_specs, out_specs=out_specs, check_vma=False)
```

profile of v0, /device:TPU:0, one launch (start us, length us, event | category | flops | bytes accessed | tf_op | source)
XLA Modules:
  0.0 43.9 jit_solution(1802645869206446881)
XLA Ops:
  0.6 0.0 copy-start
  0.6 0.9 %copy-done = f32[39,8,128]{2,1,0:T(8,128)S(1)} copy-done((f32[39,8,128]{2,1,0:T(8,128)S(1)}, f32[39,8,128]{2,1,0:T(8,128)}, u32[]{:S(2)}) %copy-start) | copy-done | bytes 159768
  1.5 0.0 copy-start.1
  1.6 0.8 %copy-done.1 = f32[4,32,128]{2,1,0:T(8,128)S(1)} copy-done((f32[4,32,128]{2,1,0:T(8,128)S(1)}, f32[4,32,128]{2,1,0:T(8,128)}, u32[]{:S(2)}) %copy-start.1) | copy-done | bytes 65560
  2.4 0.0 copy-start.2
  2.4 0.7 %copy-done.2 = f32[4,8,128]{2,1,0:T(8,128)S(1)} copy-done((f32[4,8,128]{2,1,0:T(8,128)S(1)}, f32[4,8,128]{2,1,0:T(8,128)}, u32[]{:S(2)}) %copy-start.2) | copy-done | bytes 16408
  3.1 0.0 copy-start.3
  3.1 0.7 %copy-done.3 = f32[4,8,128]{2,1,0:T(8,128)S(1)} copy-done((f32[4,8,128]{2,1,0:T(8,128)S(1)}, f32[4,8,128]{2,1,0:T(8,128)}, u32[]{:S(2)}) %copy-start.3) | copy-done | bytes 16408
  3.8 0.0 copy-start.4
  3.8 0.7 %copy-done.4 = f32[2,8,128]{2,1,0:T(8,128)S(1)} copy-done((f32[2,8,128]{2,1,0:T(8,128)S(1)}, f32[2,8,128]{2,1,0:T(8,128)}, u32[]{:S(2)}) %copy-start.4) | copy-done | bytes 8216
  4.5 0.0 copy-start.5
  4.5 0.7 %copy-done.5 = s32[8,128]{1,0:T(8,128)S(1)} copy-done((s32[8,128]{1,0:T(8,128)S(1)}, s32[8,128]{1,0:T(8,128)}, u32[]{:S(2)}) %copy-start.5) | copy-done | bytes 4120
  5.2 0.0 copy-start.6
  5.2 0.7 %copy-done.6 = s32[4,128,1]{1,2,0:T(1,128)S(1)} copy-done((s32[4,128,1]{1,2,0:T(1,128)S(1)}, s32[4,128,1]{1,2,0:T(1,128)}, u32[]{:S(2)}) %copy-start.6) | copy-done | bytes 2072
  5.9 0.0 copy-start.7
  5.9 0.7 %copy-done.7 = s32[4,128]{1,0:T(4,128)S(1)} copy-done((s32[4,128]{1,0:T(4,128)S(1)}, s32[4,128]{1,0:T(4,128)}, u32[]{:S(2)}) %copy-start.7) | copy-done | bytes 2072
  6.6 0.0 copy-start.8
  6.6 0.7 %copy-done.8 = s32[4,128]{1,0:T(4,128)S(1)} copy-done((s32[4,128]{1,0:T(4,128)S(1)}, s32[4,128]{1,0:T(4,128)}, u32[]{:S(2)}) %copy-start.8) | copy-done | bytes 2072
  7.3 35.3 %shard_map.104 = (f32[640,128]{1,0:T(8,128)S(1)}, f32[2,8]{1,0:T(2,128)S(1)}) custom-call(f32[4,32,128]{2,1,0:T(8,128)S(1)} %copy-done.1, s32[4,128]{1,0:T(4,128)S(1)} %bitcast.3, s32[4,128]{1,0:T(4,128)S(1)} %copy-done.7, s32[4,128]{1,0:T(4,128)S(1)} %copy-done.8, f32[4,8,128]{2,1,0:T(8,128)S(1)} %copy-done.2, f32[4,8,128]{2,1,0:T(8,128)S(1)} %copy-done.3, ...), custom_call_target="tpu_custom_call" | custom-call | tf_op jit(solution)/shard_map/pallas_call | solution.py:342
  42.6 0.7 %copy.13 = f32[2,40,8,128]{3,2,1,0:T(8,128)} copy(f32[2,40,8,128]{3,2,1,0:T(8,128)S(1)} %bitcast.2) | data formatting | bytes 655360
  43.3 0.6 %copy.14 = f32[2,8]{1,0:T(2,128)} copy(f32[2,8]{1,0:T(2,128)S(1)} %get-tuple-element.9) | data formatting | bytes 128
Async XLA Ops:
  0.6 0.9 %copy-start = (f32[39,8,128]{2,1,0:T(8,128)S(1)}, f32[39,8,128]{2,1,0:T(8,128)}, u32[]{:S(2)}) copy-start(f32[39,8,128]{2,1,0:T(8,128)} %diff_ref.1) | copy-start | bytes 479236
  1.5 0.8 %copy-start.1 = (f32[4,32,128]{2,1,0:T(8,128)S(1)}, f32[4,32,128]{2,1,0:T(8,128)}, u32[]{:S(2)}) copy-start(f32[4,32,128]{2,1,0:T(8,128)} %adj_ref.1) | copy-start | bytes 196612
  2.4 0.7 %copy-start.2 = (f32[4,8,128]{2,1,0:T(8,128)S(1)}, f32[4,8,128]{2,1,0:T(8,128)}, u32[]{:S(2)}) copy-start(f32[4,8,128]{2,1,0:T(8,128)} %wx_ref.1) | copy-start | bytes 49156
  3.1 0.7 %copy-start.3 = (f32[4,8,128]{2,1,0:T(8,128)S(1)}, f32[4,8,128]{2,1,0:T(8,128)}, u32[]{:S(2)}) copy-start(f32[4,8,128]{2,1,0:T(8,128)} %wy_ref.1) | copy-start | bytes 49156
  3.8 0.7 %copy-start.4 = (f32[2,8,128]{2,1,0:T(8,128)S(1)}, f32[2,8,128]{2,1,0:T(8,128)}, u32[]{:S(2)}) copy-start(f32[2,8,128]{2,1,0:T(8,128)} %prior_ref.1) | copy-start | bytes 24580
  4.5 0.7 %copy-start.5 = (s32[8,128]{1,0:T(8,128)S(1)}, s32[8,128]{1,0:T(8,128)}, u32[]{:S(2)}) copy-start(s32[8,128]{1,0:T(8,128)} %region_ref.1) | copy-start | bytes 12292
  5.2 0.7 %copy-start.6 = (s32[4,128,1]{1,2,0:T(1,128)S(1)}, s32[4,128,1]{1,2,0:T(1,128)}, u32[]{:S(2)}) copy-start(s32[4,128,1]{1,2,0:T(1,128)} %param.10) | copy-start | bytes 6148
  5.9 0.7 %copy-start.7 = (s32[4,128]{1,0:T(4,128)S(1)}, s32[4,128]{1,0:T(4,128)}, u32[]{:S(2)}) copy-start(s32[4,128]{1,0:T(4,128)} %column_ref.1) | copy-start | bytes 6148
  6.6 0.7 %copy-start.8 = (s32[4,128]{1,0:T(4,128)S(1)}, s32[4,128]{1,0:T(4,128)}, u32[]{:S(2)}) copy-start(s32[4,128]{1,0:T(4,128)} %level_ref.1) | copy-start | bytes 6148
where the time goes:
time: 44.4 us; the launch traced here: 43.9 us
  Pallas kernels  35.3 us (80%)
  local copies, waits for them, and re-layouts  7.89 us (18%)
  between operations  0.66 us (1%)
    pallas_call x1, Pallas kernels, local(): pl.pallas_call(functools.partial(kernel, dims), out_shape=(jax.ShapeDtype...  35.3 us
    unnamed x20, local copies, waits for them, and re-layouts  7.89 us

commit v1 on v0

--- a/solution.py
+++ b/solution.py
@@ -25,17 +25,14 @@
 
 def kernel(
     dims,
-    adj_ref,
-    owner_ref,
-    column_ref,
-    level_ref,
-    wx_ref,
-    wy_ref,
-    diff_ref,
-    prior_ref,
-    region_ref,
-    state,
-    grad_ref,
+    *refs,
+):
+    sources, refs = refs[:9], refs[9:]
+    state, grad_ref = refs[:2]
+    inside, refs = refs[2:11], refs[11:]
+    adj_ref, owner_ref, column_ref, level_ref, wx_ref, wy_ref, diff_ref, prior_ref, region_ref = inside
+    moves = list(zip(sources, inside))
+    (
     table,
     send,
     recv,
@@ -58,34 +55,38 @@
     halo_recv,
     g_send,
     g_recv,
-):
+    in_sem,
+    ) = refs
     nx, ny, species, levels, akl, steps, rows, cols, pixels, slots = dims
     n = nx * ny
     planes = species * levels
+    width = species * akl + 8
     gx, gy = lax.axis_index("gx"), lax.axis_index("gy")
     me = gx * ny + gy
 
-    def partner(i):
-        other = lax.rem(me + i, n)
-        return other, (lax.div(other, ny), lax.rem(other, ny))
+    def partner(dx, dy):
+        px, py = gx + dx, gy + dy
+        px = jnp.where(px >= nx, px - nx, px)
+        py = jnp.where(py >= ny, py - ny, py)
+        return px * ny + py, (px, py)
+
+    turns = [(dx, dy) for dx in range(nx) for dy in range(ny)][1:]
 
     row_in[...] = jnp.zeros(row_in.shape, F32)
     col_in[...] = jnp.zeros(col_in.shape, F32)
+    loads = [pltpu.make_async_copy(a, b, in_sem.at[i]) for i, (a, b) in enumerate(moves)]
+    for load in loads:
+        load.start()
+    table[...] = jnp.zeros(table.shape, F32)
     barrier = pltpu.get_barrier_semaphore()
 
-    def greet(i, carry):
-        other, place = partner(i)
-        pl.semaphore_signal(barrier, inc=1, device_id=place, device_id_type=MESH)
-        return carry
-
-    lax.fori_loop(1, n, greet, 0)
-
-    def pack(k):
-        table[...] = jnp.zeros((128, pixels), F32)
-        for s in range(species):
-            table[s * levels : s * levels + akl, :] = adj_ref[k, s * akl : (s + 1) * akl, :]
-        table[planes : planes + 1, :] = column_ref[k : k + 1, :].astype(F32)
-        table[planes + 1 : planes + 2, :] = level_ref[k : k + 1, :].astype(F32)
+    for turn in turns:
+        pl.semaphore_signal(barrier, inc=1, device_id=partner(*turn)[1], device_id_type=MESH)
+
+    for i in range(4):
+        loads[i].wait()
+
+    def hits_of(k):
         owner = owner_ref[k : k + 1, :].astype(F32)
         along = jnp.broadcast_to(owner, (pixels, pixels))
         down = along.T
@@ -95,48 +96,54 @@
         slot = jnp.sum(earlier, axis=0, keepdims=True)
         position = (owner * slots + slot).astype(jnp.int32)
         place = lax.broadcasted_iota(jnp.int32, (n * slots, pixels), 0)
-        hits = jnp.where(place == position, 1.0, 0.0).astype(BF16)
-        high, low = halves(table[...])
-        send[k] = dot_nt(hits, high) + dot_nt(hits, low)
-
-    def pixel_copy(k, i):
-        other, place = partner(i)
+        return jnp.where(place == position, 1.0, 0.0).astype(BF16)
+
+    def pack(t, group):
+        for i, k in enumerate(group):
+            at = width * i
+            table[t, at : at + species * akl, i * pixels : (i + 1) * pixels] = adj_ref[k]
+            at = at + species * akl
+            codes = jnp.concatenate([column_ref[k : k + 1, :], level_ref[k : k + 1, :]], axis=0)
+            table[t, at : at + 2, i * pixels : (i + 1) * pixels] = codes.astype(F32)
+        hits = jnp.concatenate([hits_of(k) for k in group], axis=1)
+        high, low = halves(table[t, :, : len(group) * pixels])
+        send[t] = dot_nt(hits, high) + dot_nt(hits, low)
+
+    def pixel_copy(t, turn):
+        other, place = partner(*turn)
         return pltpu.make_async_remote_copy(
-            src_ref=send.at[k, pl.ds(pl.multiple_of(other * slots, slots), slots)],
-            dst_ref=recv.at[k, pl.ds(pl.multiple_of(me * slots, slots), slots)],
-            send_sem=pix_send.at[k],
-            recv_sem=pix_recv.at[k],
+            src_ref=send.at[t, pl.ds(pl.multiple_of(other * slots, slots), slots)],
+            dst_ref=recv.at[t, pl.ds(pl.multiple_of(me * slots, slots), slots)],
+            send_sem=pix_send.at[t],
+            recv_sem=pix_recv.at[t],
             device_id=place,
             device_id_type=MESH,
         )
 
-    def pixel_all(k):
-        _, place = partner(1)
+    def pixel_all(t):
         part = pl.ds(0, (n - 1) * slots)
         return pltpu.make_async_remote_copy(
-            src_ref=send.at[k, part],
-            dst_ref=recv.at[k, part],
-            send_sem=pix_send.at[k],
-            recv_sem=pix_recv.at[k],
-            device_id=place,
+            src_ref=send.at[t, part],
+            dst_ref=recv.at[t, part],
+            send_sem=pix_send.at[t],
+            recv_sem=pix_recv.at[t],
+            device_id=partner(*turns[0])[1],
             device_id_type=MESH,
         )
 
-    def send_pixels(k):
-        def go(i, carry):
-            pixel_copy(k, i).start()
-            return carry
-
-        lax.fori_loop(1, n, go, 0)
+    def send_pixels(t):
+        for turn in turns:
+            pixel_copy(t, turn).start()
         mine = pl.ds(pl.multiple_of(me * slots, slots), slots)
-        recv[k, mine, :] = send[k, mine, :]
-
-    pack(steps - 1)
+        recv[t, mine, :] = send[t, mine, :]
+
+    pack(0, (steps - 1,))
     pl.semaphore_wait(barrier, n - 1)
-    send_pixels(steps - 1)
-    for k in reversed(range(steps - 1)):
-        pack(k)
-        send_pixels(k)
+    send_pixels(0)
+    pack(1, tuple(range(steps - 1)))
+    send_pixels(1)
+    for load in loads[4:]:
+        load.wait()
 
     ratio = jnp.zeros((rows, cols), F32)
     for level in range(levels):
@@ -154,16 +161,23 @@
     lane = lax.broadcasted_iota(jnp.int32, (rows, cols), 1)
     sub = lax.broadcasted_iota(jnp.int32, (rows, cols), 0)
 
-    def spread(k):
-        pixel_all(k).wait_recv()
+    def spread(t, k):
+        if t == 0:
+            pixel_all(0).wait_recv()
         total = [None] * rows
         chunk = min(256, n * slots)
         for first in range(0, n * slots, chunk):
-            got = recv[k, first : first + chunk, :]
+            got = recv[t, first : first + chunk, :]
+            if t:
+                got = pltpu.roll(got, lax.rem(128 - width * k, 128), 1)
             spot = lax.broadcasted_iota(jnp.int32, got.shape, 1)
-            column = jnp.broadcast_to(got[:, planes : planes + 1], got.shape).astype(jnp.int32)
-            level = jnp.broadcast_to(got[:, planes + 1 : planes + 2], got.shape).astype(jnp.int32)
-            profile = jnp.where(spot < planes, got, 0.0)
+            column = jnp.broadcast_to(got[:, width - 8 : width - 7], got.shape).astype(jnp.int32)
+            level = jnp.broadcast_to(got[:, width - 7 : width - 6], got.shape).astype(jnp.int32)
+            profile = jnp.where(spot < akl, got, 0.0)
+            for s in range(1, species):
+                place = s * levels
+                there = (spot >= place) & (spot < place + akl)
+                profile = jnp.where(there, pltpu.roll(got, place - s * akl, 1), profile)
             bit = 1
             while bit <= levels - akl:
                 profile = jnp.where((level & bit) != 0, pltpu.roll(profile, bit, 1), profile)
@@ -206,7 +220,7 @@
             device_id_type=MESH,
         )
 
-    spread(steps - 1)
+    spread(0, 0)
 
     def step(turn, carry):
         k = steps - 1 - turn
@@ -245,7 +259,8 @@
 
         @pl.when(k > 0)
         def _():
-            spread(jnp.maximum(k - 1, 0))
+            pl.when(k == steps - 1)(lambda: pixel_all(1).wait_recv())
+            spread(1, jnp.maximum(k - 1, 0))
 
         for side in range(4):
             pl.when(comes[side])(lambda side=side: halo(k, side).wait_recv())
@@ -291,34 +306,28 @@
     high, low = halves(jnp.concatenate(parts, axis=1))
     gsend[...] = (dot_nt(hits, high) + dot_nt(hits, low)).reshape(n, 1, 128)
 
-    def grad_copy(i):
-        other, place = partner(i)
-        return pltpu.make_async_remote_copy(
+    for turn in turns:
+        other, place = partner(*turn)
+        pltpu.make_async_remote_copy(
             src_ref=gsend.at[other],
             dst_ref=grecv.at[me],
             send_sem=g_send,
             recv_sem=g_recv,
             device_id=place,
             device_id_type=MESH,
-        )
-
-    def go(i, carry):
-        grad_copy(i).start()
-        return carry
-
-    lax.fori_loop(1, n, go, 0)
+        ).start()
     grecv[me] = gsend[me]
+    for t in range(2):
+        pixel_all(t).wait_send()
     for k in range(steps):
-        pixel_all(k).wait_send()
         for side in range(4):
             pl.when(has[side])(lambda side=side, k=k: halo(k, side).wait_send())
-    _, place = partner(1)
     everything = pltpu.make_async_remote_copy(
         src_ref=gsend.at[pl.ds(0, n - 1)],
         dst_ref=grecv.at[pl.ds(0, n - 1)],
         send_sem=g_send,
         recv_sem=g_recv,
-        device_id=place,
+        device_id=partner(*turns[0])[1],
         device_id_type=MESH,
     )
     everything.wait_send()
@@ -339,18 +348,20 @@
     dims = (nx, ny, species, levels, akl, steps, rows, cols, pixels, slots)
     vmem = pl.BlockSpec(memory_space=pltpu.VMEM)
     tile = (planes * rows, cols)
+    operands = (adj, owner.reshape(steps, pixels), column, level, wx, wy, diff, prior, region)
     state, grad = pl.pallas_call(
         functools.partial(kernel, dims),
         out_shape=(
             jax.ShapeDtypeStruct(tile, F32),
             jax.ShapeDtypeStruct((species, REG_DEV), F32),
         ),
-        in_specs=[vmem] * 9,
+        in_specs=[pl.BlockSpec(memory_space=pltpu.HBM)] * 9,
         out_specs=(vmem, vmem),
         scratch_shapes=[
-            pltpu.VMEM((128, pixels), F32),
-            pltpu.VMEM((steps, n * slots, 128), F32),
-            pltpu.VMEM((steps, n * slots, 128), F32),
+            *[pltpu.VMEM(a.shape, a.dtype) for a in operands],
+            pltpu.VMEM((2, 128, (steps - 1) * pixels), F32),
+            pltpu.VMEM((2, n * slots, 128), F32),
+            pltpu.VMEM((2, n * slots, 128), F32),
             pltpu.VMEM((levels * rows, cols), F32),
             pltpu.VMEM((levels * rows, cols), F32),
             pltpu.VMEM((levels * rows, cols), F32),
@@ -364,17 +375,18 @@
             pltpu.VMEM((species, rows, cols), F32),
             pltpu.VMEM((n, 1, 128), F32),
             pltpu.VMEM((n, 1, 128), F32),
-            pltpu.SemaphoreType.DMA((steps,)),
-            pltpu.SemaphoreType.DMA((steps,)),
+            pltpu.SemaphoreType.DMA((2,)),
+            pltpu.SemaphoreType.DMA((2,)),
             pltpu.SemaphoreType.DMA((steps, 4)),
             pltpu.SemaphoreType.DMA((steps, 4)),
             pltpu.SemaphoreType.DMA,
             pltpu.SemaphoreType.DMA,
+            pltpu.SemaphoreType.DMA((9,)),
         ],
         compiler_params=pltpu.CompilerParams(
             collective_id=0, has_side_effects=True, vmem_limit_bytes=40 * 1024 * 1024
         ),
-    )(adj, owner.reshape(steps, pixels), column, level, wx, wy, diff, prior, region)
+    )(*operands)
     return state.reshape(species, levels, rows, cols), grad
 
 

time: 44.4 us -> 42 us (0.946)
  Pallas kernels: 35.3 us -> 33 us
    pallas_call x1, Pallas kernels: 35.3 us -> 33 us  [local(): pl.pallas_call(functools.partial(kernel, dims), out_shape=(jax.ShapeDtype...]
where the time goes in v1:
time: 42 us; the launch traced here: 41.5 us
  Pallas kernels  33 us (79%)
  local copies, waits for them, and re-layouts  7.89 us (19%)
  between operations  0.66 us (2%)
    pallas_call x1, Pallas kernels, local(): pl.pallas_call(functools.partial(kernel, dims), out_shape=(jax.ShapeDtype...  33 us
    unnamed x20, local copies, waits for them, and re-layouts  7.89 us

profile of v1, /device:TPU:0, one launch (start us, length us, event | category | flops | bytes accessed | tf_op | source)
XLA Modules:
  0.0 41.5 jit_solution(550442622978921375)
XLA Ops:
  0.6 0.0 copy-start
  0.6 0.9 %copy-done = f32[39,8,128]{2,1,0:T(8,128)S(1)} copy-done((f32[39,8,128]{2,1,0:T(8,128)S(1)}, f32[39,8,128]{2,1,0:T(8,128)}, u32[]{:S(2)}) %copy-start) | copy-done | bytes 159768
  1.5 0.0 copy-start.1
  1.6 0.8 %copy-done.1 = f32[4,32,128]{2,1,0:T(8,128)S(1)} copy-done((f32[4,32,128]{2,1,0:T(8,128)S(1)}, f32[4,32,128]{2,1,0:T(8,128)}, u32[]{:S(2)}) %copy-start.1) | copy-done | bytes 65560
  2.4 0.0 copy-start.2
  2.4 0.7 %copy-done.2 = f32[4,8,128]{2,1,0:T(8,128)S(1)} copy-done((f32[4,8,128]{2,1,0:T(8,128)S(1)}, f32[4,8,128]{2,1,0:T(8,128)}, u32[]{:S(2)}) %copy-start.2) | copy-done | bytes 16408
  3.1 0.0 copy-start.3
  3.1 0.7 %copy-done.3 = f32[4,8,128]{2,1,0:T(8,128)S(1)} copy-done((f32[4,8,128]{2,1,0:T(8,128)S(1)}, f32[4,8,128]{2,1,0:T(8,128)}, u32[]{:S(2)}) %copy-start.3) | copy-done | bytes 16408
  3.8 0.0 copy-start.4
  3.8 0.7 %copy-done.4 = f32[2,8,128]{2,1,0:T(8,128)S(1)} copy-done((f32[2,8,128]{2,1,0:T(8,128)S(1)}, f32[2,8,128]{2,1,0:T(8,128)}, u32[]{:S(2)}) %copy-start.4) | copy-done | bytes 8216
  4.5 0.0 copy-start.5
  4.5 0.7 %copy-done.5 = s32[8,128]{1,0:T(8,128)S(1)} copy-done((s32[8,128]{1,0:T(8,128)S(1)}, s32[8,128]{1,0:T(8,128)}, u32[]{:S(2)}) %copy-start.5) | copy-done | bytes 4120
  5.2 0.0 copy-start.6
  5.2 0.7 %copy-done.6 = s32[4,128,1]{1,2,0:T(1,128)S(1)} copy-done((s32[4,128,1]{1,2,0:T(1,128)S(1)}, s32[4,128,1]{1,2,0:T(1,128)}, u32[]{:S(2)}) %copy-start.6) | copy-done | bytes 2072
  5.9 0.0 copy-start.7
  5.9 0.7 %copy-done.7 = s32[4,128]{1,0:T(4,128)S(1)} copy-done((s32[4,128]{1,0:T(4,128)S(1)}, s32[4,128]{1,0:T(4,128)}, u32[]{:S(2)}) %copy-start.7) | copy-done | bytes 2072
  6.6 0.0 copy-start.8
  6.6 0.7 %copy-done.8 = s32[4,128]{1,0:T(4,128)S(1)} copy-done((s32[4,128]{1,0:T(4,128)S(1)}, s32[4,128]{1,0:T(4,128)}, u32[]{:S(2)}) %copy-start.8) | copy-done | bytes 2072
  7.3 33.0 %shard_map.104 = (f32[640,128]{1,0:T(8,128)S(1)}, f32[2,8]{1,0:T(2,128)S(1)}) custom-call(f32[4,32,128]{2,1,0:T(8,128)S(1)} %copy-done.1, s32[4,128]{1,0:T(4,128)S(1)} %bitcast.3, s32[4,128]{1,0:T(4,128)S(1)} %copy-done.7, s32[4,128]{1,0:T(4,128)S(1)} %copy-done.8, f32[4,8,128]{2,1,0:T(8,128)S(1)} %copy-done.2, f32[4,8,128]{2,1,0:T(8,128)S(1)} %copy-done.3, ...), custom_call_target="tpu_custom_call" | custom-call | tf_op jit(solution)/shard_map/pallas_call | solution.py:352
  40.2 0.7 %copy.13 = f32[2,40,8,128]{3,2,1,0:T(8,128)} copy(f32[2,40,8,128]{3,2,1,0:T(8,128)S(1)} %bitcast.2) | data formatting | bytes 655360
  41.0 0.6 %copy.14 = f32[2,8]{1,0:T(2,128)} copy(f32[2,8]{1,0:T(2,128)S(1)} %get-tuple-element.9) | data formatting | bytes 128
Async XLA Ops:
  0.6 0.9 %copy-start = (f32[39,8,128]{2,1,0:T(8,128)S(1)}, f32[39,8,128]{2,1,0:T(8,128)}, u32[]{:S(2)}) copy-start(f32[39,8,128]{2,1,0:T(8,128)} %refs_6_.1) | copy-start | bytes 479236
  1.5 0.8 %copy-start.1 = (f32[4,32,128]{2,1,0:T(8,128)S(1)}, f32[4,32,128]{2,1,0:T(8,128)}, u32[]{:S(2)}) copy-start(f32[4,32,128]{2,1,0:T(8,128)} %refs_0_.1) | copy-start | bytes 196612
  2.4 0.7 %copy-start.2 = (f32[4,8,128]{2,1,0:T(8,128)S(1)}, f32[4,8,128]{2,1,0:T(8,128)}, u32[]{:S(2)}) copy-start(f32[4,8,128]{2,1,0:T(8,128)} %refs_4_.1) | copy-start | bytes 49156
  3.1 0.7 %copy-start.3 = (f32[4,8,128]{2,1,0:T(8,128)S(1)}, f32[4,8,128]{2,1,0:T(8,128)}, u32[]{:S(2)}) copy-start(f32[4,8,128]{2,1,0:T(8,128)} %refs_5_.1) | copy-start | bytes 49156
  3.8 0.7 %copy-start.4 = (f32[2,8,128]{2,1,0:T(8,128)S(1)}, f32[2,8,128]{2,1,0:T(8,128)}, u32[]{:S(2)}) copy-start(f32[2,8,128]{2,1,0:T(8,128)} %refs_7_.1) | copy-start | bytes 24580
  4.5 0.7 %copy-start.5 = (s32[8,128]{1,0:T(8,128)S(1)}, s32[8,128]{1,0:T(8,128)}, u32[]{:S(2)}) copy-start(s32[8,128]{1,0:T(8,128)} %refs_8_.1) | copy-start | bytes 12292
  5.2 0.7 %copy-start.6 = (s32[4,128,1]{1,2,0:T(1,128)S(1)}, s32[4,128,1]{1,2,0:T(1,128)}, u32[]{:S(2)}) copy-start(s32[4,128,1]{1,2,0:T(1,128)} %param.10) | copy-start | bytes 6148
  5.9 0.7 %copy-start.7 = (s32[4,128]{1,0:T(4,128)S(1)}, s32[4,128]{1,0:T(4,128)}, u32[]{:S(2)}) copy-start(s32[4,128]{1,0:T(4,128)} %refs_2_.1) | copy-start | bytes 6148
  6.6 0.7 %copy-start.8 = (s32[4,128]{1,0:T(4,128)S(1)}, s32[4,128]{1,0:T(4,128)}, u32[]{:S(2)}) copy-start(s32[4,128]{1,0:T(4,128)} %refs_3_.1) | copy-start | bytes 6148

commit v2 on v1

--- a/solution.py
+++ b/solution.py
@@ -384,7 +384,7 @@
             pltpu.SemaphoreType.DMA((9,)),
         ],
         compiler_params=pltpu.CompilerParams(
-            collective_id=0, has_side_effects=True, vmem_limit_bytes=40 * 1024 * 1024
+            collective_id=0, has_side_effects=True, vmem_limit_bytes=56 * 1024 * 1024
         ),
     )(*operands)
     return state.reshape(species, levels, rows, cols), grad

time: 42 us -> 36.3 us (0.86)
  local copies, waits for them, and re-layouts: 7.89 us -> 2.29 us
    unnamed x20 -> x4, local copies, waits for them, and re-layouts: 7.89 us -> 2.29 us
where the time goes in v2:
time: 36.3 us; the launch traced here: 36.2 us
  Pallas kernels  33.2 us (91%)
  local copies, waits for them, and re-layouts  2.29 us (6%)
  between operations  0.65 us (2%)
    pallas_call x1, Pallas kernels, local(): pl.pallas_call(functools.partial(kernel, dims), out_shape=(jax.ShapeDtype...  33.2 us
    unnamed x4, local copies, waits for them, and re-layouts  2.29 us

profile of v2, /device:TPU:0, one launch (start us, length us, event | category | flops | bytes accessed | tf_op | source)
XLA Modules:
  0.0 36.2 jit_solution(12180754252876130291)
XLA Ops:
  0.6 33.2 %shard_map.104 = (f32[640,128]{1,0:T(8,128)}, f32[2,8]{1,0:T(2,128)}) custom-call(f32[4,32,128]{2,1,0:T(8,128)} %refs_0_.1, s32[4,128]{1,0:T(4,128)} %bitcast.3, s32[4,128]{1,0:T(4,128)} %refs_2_.1, s32[4,128]{1,0:T(4,128)} %refs_3_.1, f32[4,8,128]{2,1,0:T(8,128)} %refs_4_.1, f32[4,8,128]{2,1,0:T(8,128)} %refs_5_.1, f32[39,8,128]{2,1,0:T(8,128)} %refs_6_.1, ...), custom_call_target="tpu_custom_call" | custom-call | tf_op jit(solution)/shard_map/pallas_call | solution.py:352
  33.9 0.0 copy-start
  33.9 1.7 %copy.13 = f32[2,40,8,128]{3,2,1,0:T(8,128)} copy(f32[2,40,8,128]{3,2,1,0:T(8,128)} %bitcast.2) | data formatting | bytes 655360
  35.6 0.0 copy-done
  35.6 0.6 %copy.14 = f32[2,8]{1,0:T(2,128)} copy(f32[2,8]{1,0:T(2,128)S(1)} %copy-done) | data formatting | bytes 128
Async XLA Ops:
  33.9 1.7 %copy-start = (f32[2,8]{1,0:T(2,128)S(1)}, f32[2,8]{1,0:T(2,128)}, u32[]{:S(2)}) copy-start(f32[2,8]{1,0:T(2,128)} %get-tuple-element.9) | copy-start | bytes 196

commit v3 on v2

--- a/solution.py
+++ b/solution.py
@@ -56,6 +56,7 @@
     g_send,
     g_recv,
     in_sem,
+    owners,
     ) = refs
     nx, ny, species, levels, akl, steps, rows, cols, pixels, slots = dims
     n = nx * ny
@@ -77,12 +78,12 @@
     loads = [pltpu.make_async_copy(a, b, in_sem.at[i]) for i, (a, b) in enumerate(moves)]
     for load in loads:
         load.start()
-    table[...] = jnp.zeros(table.shape, F32)
     barrier = pltpu.get_barrier_semaphore()
 
     for turn in turns:
         pl.semaphore_signal(barrier, inc=1, device_id=partner(*turn)[1], device_id_type=MESH)
 
+    table[...] = jnp.zeros(table.shape, F32)
     for i in range(4):
         loads[i].wait()
 
@@ -142,19 +143,28 @@
     send_pixels(0)
     pack(1, tuple(range(steps - 1)))
     send_pixels(1)
+    def factor():
+        ratio = jnp.zeros((rows, cols), F32)
+        for level in range(levels):
+            below = diff_ref[level - 1] if level else jnp.zeros((rows, cols), F32)
+            above = diff_ref[level] if level < levels - 1 else jnp.zeros((rows, cols), F32)
+            inverse = 1.0 / (1.0 + below + above + below * ratio)
+            ratio = -above * inverse
+            here = slice(level * rows, (level + 1) * rows)
+            inv_ref[here, :] = inverse
+            coup_ref[here, :] = below * inverse
+            ratio_ref[here, :] = ratio
+
+    def region_owners():
+        device = lax.broadcasted_iota(jnp.int32, (n, cols), 0)
+        for x in range(0, rows, 2):
+            owner = lax.shift_right_logical(region_ref[x : x + 1], 3)
+            hits = jnp.where(device == owner, 1.0, 0.0).astype(BF16)
+            owners[:, x // 2 * cols : (x // 2 + 1) * cols] = hits
+
     for load in loads[4:]:
         load.wait()
 
-    ratio = jnp.zeros((rows, cols), F32)
-    for level in range(levels):
-        below = diff_ref[level - 1] if level else jnp.zeros((rows, cols), F32)
-        above = diff_ref[level] if level < levels - 1 else jnp.zeros((rows, cols), F32)
-        inverse = 1.0 / (1.0 + below + above + below * ratio)
-        ratio = -above * inverse
-        here = slice(level * rows, (level + 1) * rows)
-        inv_ref[here, :] = inverse
-        coup_ref[here, :] = below * inverse
-        ratio_ref[here, :] = ratio
     surf[...] = jnp.zeros(surf.shape, F32)
     state[...] = jnp.zeros(state.shape, F32)
 
@@ -259,6 +269,8 @@
 
         @pl.when(k > 0)
         def _():
+            pl.when(k == steps - 1)(factor)
+            pl.when(k == steps - 2)(region_owners)
             pl.when(k == steps - 1)(lambda: pixel_all(1).wait_recv())
             spread(1, jnp.maximum(k - 1, 0))
 
@@ -291,18 +303,16 @@
     lax.fori_loop(0, steps, step, 0)
 
     region = region_ref[...]
-    hits, parts = [], []
+    parts = []
     sums = [surf[s] + pltpu.roll(surf[s], rows - 1, 0) for s in range(species)]
     for x in range(0, rows, 2):
         reg = region[x : x + 1]
-        owner = lax.broadcasted_iota(jnp.int32, (n, cols), 0)
-        hits.append(jnp.where(owner == lax.shift_right_logical(reg, 3), 1.0, 0.0).astype(BF16))
         place = lax.broadcasted_iota(jnp.int32, (REG_DEV, cols), 0)
         same = place == (reg & (REG_DEV - 1))
         blocks = [jnp.where(same, sums[s][x : x + 1], 0.0) for s in range(species)]
         blocks.append(jnp.zeros((128 - species * REG_DEV, cols), F32))
         parts.append(jnp.concatenate(blocks, axis=0))
-    hits = jnp.concatenate(hits, axis=1)
+    hits = owners[...]
     high, low = halves(jnp.concatenate(parts, axis=1))
     gsend[...] = (dot_nt(hits, high) + dot_nt(hits, low)).reshape(n, 1, 128)
 
@@ -382,6 +392,7 @@
             pltpu.SemaphoreType.DMA,
             pltpu.SemaphoreType.DMA,
             pltpu.SemaphoreType.DMA((9,)),
+            pltpu.VMEM((n, rows // 2 * cols), BF16),
         ],
         compiler_params=pltpu.CompilerParams(
             collective_id=0, has_side_effects=True, vmem_limit_bytes=56 * 1024 * 1024

time: 36.3 us -> 36.3 us (level)
  no operation moved by 1% of the time
where the time goes in v3:
time: 36.3 us; the launch traced here: 36.2 us
  Pallas kernels  33.2 us (91%)
  local copies, waits for them, and re-layouts  2.29 us (6%)
  between operations  0.65 us (2%)
    pallas_call x1, Pallas kernels, local(): pl.pallas_call(functools.partial(kernel, dims), out_shape=(jax.ShapeDtype...  33.2 us
    unnamed x4, local copies, waits for them, and re-layouts  2.29 us

profile of v3, /device:TPU:0, one launch (start us, length us, event | category | flops | bytes accessed | tf_op | source)
XLA Modules:
  0.0 36.2 jit_solution(5770136162912330046)
XLA Ops:
  0.6 33.2 %shard_map.104 = (f32[640,128]{1,0:T(8,128)}, f32[2,8]{1,0:T(2,128)}) custom-call(f32[4,32,128]{2,1,0:T(8,128)} %refs_0_.1, s32[4,128]{1,0:T(4,128)} %bitcast.3, s32[4,128]{1,0:T(4,128)} %refs_2_.1, s32[4,128]{1,0:T(4,128)} %refs_3_.1, f32[4,8,128]{2,1,0:T(8,128)} %refs_4_.1, f32[4,8,128]{2,1,0:T(8,128)} %refs_5_.1, f32[39,8,128]{2,1,0:T(8,128)} %refs_6_.1, ...), custom_call_target="tpu_custom_call" | custom-call | tf_op jit(solution)/shard_map/pallas_call | solution.py:362
  33.9 0.0 copy-start
  33.9 1.7 %copy.13 = f32[2,40,8,128]{3,2,1,0:T(8,128)} copy(f32[2,40,8,128]{3,2,1,0:T(8,128)} %bitcast.2) | data formatting | bytes 655360
  35.6 0.0 copy-done
  35.6 0.6 %copy.14 = f32[2,8]{1,0:T(2,128)} copy(f32[2,8]{1,0:T(2,128)S(1)} %copy-done) | data formatting | bytes 128
Async XLA Ops:
  33.9 1.7 %copy-start = (f32[2,8]{1,0:T(2,128)S(1)}, f32[2,8]{1,0:T(2,128)}, u32[]{:S(2)}) copy-start(f32[2,8]{1,0:T(2,128)} %get-tuple-element.9) | copy-start | bytes 196

commit v4 on v3

--- a/solution.py
+++ b/solution.py
@@ -139,9 +139,9 @@
         recv[t, mine, :] = send[t, mine, :]
 
     pack(0, (steps - 1,))
+    pack(1, tuple(range(steps - 1)))
     pl.semaphore_wait(barrier, n - 1)
     send_pixels(0)
-    pack(1, tuple(range(steps - 1)))
     send_pixels(1)
     def factor():
         ratio = jnp.zeros((rows, cols), F32)

time: 36.3 us -> 36.3 us (level)
  no operation moved by 1% of the time
where the time goes in v4:
time: 36.3 us; the launch traced here: 36.2 us
  Pallas kernels  33.2 us (91%)
  local copies, waits for them, and re-layouts  2.29 us (6%)
  between operations  0.65 us (2%)
    pallas_call x1, Pallas kernels, local(): pl.pallas_call(functools.partial(kernel, dims), out_shape=(jax.ShapeDtype...  33.2 us
    unnamed x4, local copies, waits for them, and re-layouts  2.29 us

profile of v4, /device:TPU:0, one launch (start us, length us, event | category | flops | bytes accessed | tf_op | source)
XLA Modules:
  0.0 36.2 jit_solution(59921835225450765)
XLA Ops:
  0.6 33.2 %shard_map.104 = (f32[640,128]{1,0:T(8,128)}, f32[2,8]{1,0:T(2,128)}) custom-call(f32[4,32,128]{2,1,0:T(8,128)} %refs_0_.1, s32[4,128]{1,0:T(4,128)} %bitcast.3, s32[4,128]{1,0:T(4,128)} %refs_2_.1, s32[4,128]{1,0:T(4,128)} %refs_3_.1, f32[4,8,128]{2,1,0:T(8,128)} %refs_4_.1, f32[4,8,128]{2,1,0:T(8,128)} %refs_5_.1, f32[39,8,128]{2,1,0:T(8,128)} %refs_6_.1, ...), custom_call_target="tpu_custom_call" | custom-call | tf_op jit(solution)/shard_map/pallas_call | solution.py:362
  33.9 0.0 copy-start
  33.9 1.7 %copy.13 = f32[2,40,8,128]{3,2,1,0:T(8,128)} copy(f32[2,40,8,128]{3,2,1,0:T(8,128)} %bitcast.2) | data formatting | bytes 655360
  35.6 0.0 copy-done
  35.6 0.6 %copy.14 = f32[2,8]{1,0:T(2,128)} copy(f32[2,8]{1,0:T(2,128)S(1)} %copy-done) | data formatting | bytes 128
Async XLA Ops:
  33.9 1.7 %copy-start = (f32[2,8]{1,0:T(2,128)S(1)}, f32[2,8]{1,0:T(2,128)}, u32[]{:S(2)}) copy-start(f32[2,8]{1,0:T(2,128)} %get-tuple-element.9) | copy-start | bytes 196
